TPU v7x, 512 devices: a whole 4x4x16 slice. The times are simulated.
512 devices in a mesh: orb: 8 (over y, x_lo), grid: 64 (over x_hi, z, core).
Axes of the slice: x: 4 (x_hi: 2, x_lo: 2; x = x_hi * 2 + x_lo), y: 4, z: 16, core: 2. Of those that a mesh axis runs over, the one named last changes fastest.
Arguments:
- random_orbitals: float32 [8, 256, 256, 256], P('orb', 'grid'), may hold values from -6 to 6
- potential: float32 [256, 256, 256], P('grid'), may hold values from -1.5 to 0.5
- sphere_cells: int32 [1024, 2, 128], P('grid'), may hold values from 0 to 65535, as said below
- projectors: float32 [1024, 4, 128], P('grid'), may hold values from -0.9 to 0.9
- kb_energy: float32 [4], replicated, may hold values from 0.5 to 1.5
- cheb_coef: float32 [3], replicated, may hold values from 0.5 to 1.5
Outputs:
- density: float32 [256, 256, 256], P('grid')
Inputs may be any that keep to these rules, and one draw needn't show every extreme that they name: `sphere_cells`: for each atom a the 128 points are distinct cells: the 128 offsets (dz, dy, dx) with |dz|, |dy|, |dx| <= 3 nearest to the atom's centre, ties broken by the order of (dz, dy, dx) from smallest to largest, added to the centre with periodic wrap along each dimension; row 0 holds the z-plane and row 1 the cell y * 256 + x. The centre's z lies in the slab of planes (a // 16) * 4 to (a // 16) * 4 + 3. Spheres of different atoms may share cells.
All inputs are finite; a program needn't handle non-finite values.
Results may differ from a plain program's by a relative error of at most 0.0002.
Values sent between devices are 32-bit elements; how exact they have to be, the bound alone decides.
A program may use at most 64 MiB of HBM per device.

v0:
```python
import math
import jax
import jax.numpy as jnp
from jax import lax
from jax.sharding import PartitionSpec as P

REACH = 3
PRECISE = lax.Precision.HIGHEST
CENTRE = 2.0
HALF_RANGE = 4.0


def with_halo(cells, sides, width):
    for axis, dim in sides:
        count = lax.axis_size(axis)
        head = lax.slice_in_dim(cells, 0, width, axis=dim)
        tail = lax.slice_in_dim(cells, cells.shape[dim] - width, cells.shape[dim], axis=dim)
        cells = jnp.concatenate(
            [
                lax.ppermute(tail, axis, [(i, (i + 1) % count) for i in range(count)]),
                cells,
                lax.ppermute(head, axis, [((i + 1) % count, i) for i in range(count)]),
            ],
            axis=dim,
        )
    return cells


def from_behind(block, axis, distance):
    devices = range(lax.axis_size(axis))
    route = [((i - distance) % len(devices), i) for i in devices]
    return lax.ppermute(block, axis, route)


def kinetic_table(length):
    places = jnp.arange(length)
    offset = places[:, None] - places[None, :]
    parity = jnp.where(offset % 2 == 0, 1.0, -1.0).astype(jnp.float32)
    angle_half = offset.astype(jnp.float32) * (math.pi / length)
    sine = jnp.where(offset == 0, 1.0, jnp.sin(angle_half))
    off_diag = parity / (2.0 * sine * sine)
    on_diag = jnp.float32(length * length / 12.0 + 1.0 / 6.0)
    return jnp.where(offset == 0, on_diag, off_diag) * (4.0 / (length * length))


def local(random_orbitals, potential, sphere_cells, projectors, kb_energy, cheb_coef):
    grid_count = lax.axis_size("grid")
    grid_pos = lax.axis_index("grid")
    planes = potential.shape[0]
    rows_y = potential.shape[1]
    cols_x = potential.shape[2]
    all_planes = planes * grid_count
    plane_cells = rows_y * cols_x
    first_plane = grid_pos * planes
    orb_count = random_orbitals.shape[0]
    per_dev = sphere_cells.shape[0]
    kinetic_x = kinetic_table(cols_x)
    kinetic_y = kinetic_table(rows_y)
    kinetic_z = kinetic_table(all_planes)

    def along_z(columns):
        turned = jnp.einsum("ozyx,zw->owyx", columns, kinetic_z, precision=PRECISE)
        return lax.all_to_all(turned, "grid", split_axis=1, concat_axis=2, tiled=True)

    z_glob = sphere_cells[:, 0, :]
    in_plane = sphere_cells[:, 1, :]
    local_plane = (z_glob - first_plane + REACH) % all_planes
    ghost_index = (local_plane * plane_cells + in_plane).reshape(-1)

    def nonlocal_term(vector):
        extended = with_halo(vector, (("grid", 1),), REACH)
        flattened = extended.reshape(orb_count, -1)
        values = flattened[:, ghost_index].reshape(orb_count, per_dev, -1)
        coeffs = jnp.einsum("oaj,apj->oap", values, projectors, precision=PRECISE) * kb_energy
        spread = jnp.einsum("oap,apj->oaj", coeffs, projectors, precision=PRECISE).reshape(
            orb_count, -1
        )
        placed = jnp.zeros_like(flattened).at[:, ghost_index].add(spread).reshape(extended.shape)
        lower_rim = placed[:, :REACH]
        upper_rim = placed[:, REACH + planes :]
        from_above = from_behind(lower_rim, "grid", -1)
        from_below = from_behind(upper_rim, "grid", 1)
        interior = placed[:, REACH : REACH + planes]
        interior = interior.at[:, :REACH].add(from_below)
        interior = interior.at[:, planes - REACH :].add(from_above)
        return interior

    def apply_hamiltonian(vector):
        kinetic = jnp.dot(vector.reshape(-1, cols_x), kinetic_x, precision=PRECISE).reshape(
            vector.shape
        )
        kinetic = kinetic + jnp.einsum("ozyx,yw->ozwx", vector, kinetic_y, precision=PRECISE)
        kinetic = kinetic + along_z(
            lax.all_to_all(vector, "grid", split_axis=2, concat_axis=1, tiled=True)
        )
        summed = kinetic + potential * vector + nonlocal_term(vector)
        return (summed - CENTRE * vector) / HALF_RANGE

    first_term = apply_hamiltonian(random_orbitals)
    second_term = 2.0 * apply_hamiltonian(first_term) - random_orbitals
    filtered = (
        cheb_coef[0] * random_orbitals + cheb_coef[1] * first_term + cheb_coef[2] * second_term
    )
    group_density = jnp.sum(filtered * filtered, axis=0)
    density = lax.psum(group_density, "orb")
    return density / (orb_count * lax.axis_size("orb"))


def solution(mesh):
    in_specs = (
        P("orb", "grid", None, None),
        P("grid", None, None),
        P("grid", None, None),
        P("grid", None, None),
        P(),
        P(),
    )
    out_specs = P("grid", None, None)
    return jax.shard_map(local, mesh=mesh, in_specs=in_specs, out_specs=out_specs, check_vma=False)
```

profile of v0, /device:TPU:4, one launch (start us, length us, event | category | flops | bytes accessed | tf_op | source)
XLA Modules:
  0.0 507.4 jit_solution(14557212406994386126)
XLA Ops:
  6.5 1.9 copy.20
  8.4 70.6 %all_to_all.66 = f32[1,4,256,256]{3,1,0,2:T(4,128)S(1)} all-to-all(f32[1,4,256,256]{3,1,0,2:T(4,128)S(1)} %copy.20), channel_id=1, replica_groups=mesh['orb'=8,'grid'=64] {'grid'}, dimensions={2} | all-to-all | bytes 2097152 | tf_op jit(solution)/shard_map/all_to_all | solution.py:94
  79.6 2.1 convolution_bitcast_fusion.3
  81.7 1.6 copy.22
  83.3 9.8 %all-to-all-start.1 = ((f32[1,256,4,256]{3,2,0,1:T(4,128)}), f32[1,256,4,256]{3,2,0,1:T(4,128)}, u32[]{:S(2)}, u32[]{:S(2)}) async-start(f32[1,256,4,256]{3,2,0,1:T(4,128)} %copy.22), calls=%async_computation.1 | async-start | bytes 2097152 | tf_op jit(solution)/shard_map/all_to_all | solution.py:63
  93.1 1.0 fusion.111
  94.1 2.0 collective-permute-start
  96.2 7.1 %collective-permute-start.1 = (f32[1,3,256,256]{3,2,1,0:T(8,128)S(1)}, f32[1,3,256,256]{3,2,1,0:T(8,128)S(1)}, u32[]{:S(2)}, u32[]{:S(2)}) collective-permute-start(f32[1,3,256,256]{3,2,1,0:T(8,128)S(1)} %get-tuple-element.60), channel_id=1, source_target_pairs={{1,0},{2,1},{3,2},{4,3},{5,4},{6,5},{7,6},{8,7},{9,8},{10,9},{11,1... | collective-permute-start | bytes 2359304 | tf_op jit(solution)/shard_map/ppermute | solution.py:22
  103.4 46.4 %collective-permute-done = f32[1,3,256,256]{3,2,1,0:T(8,128)S(1)} collective-permute-done((f32[1,3,256,256]{3,2,1,0:T(8,128)}, f32[1,3,256,256]{3,2,1,0:T(8,128)S(1)}, u32[]{:S(2)}, u32[]{:S(2)}) %collective-permute-start) | collective-permute-done | bytes 786464 | tf_op jit(solution)/shard_map/ppermute | solution.py:20
  150.0 1.3 copy.40
  151.3 11.8 %gather_fusion = f32[2048]{0:T(1024)S(1)} fusion(f32[655360]{0:T(1024)S(1)} %bitcast.161, s32[2048]{0:T(1024)S(1)} %broadcast_clamp_fusion), kind=kCustom, calls=%fused_computation | custom fusion | bytes 24576 | tf_op jit(solution)/shard_map/gather | solution.py:73
  163.7 11.9 %scatter_custom_fusion = f32[655360]{0:T(1024)S(1)} fusion(s32[2048]{0:T(1024)S(1)} %bitcast.173, f32[2048]{0:T(1024)S(1)} %bitcast.182, f32[]{:T(128)} %constant.158.clone.1), kind=kCustom, calls=%fused_computation.14 | custom fusion | flops 2048 | bytes 2621444 | tf_op jit(solution)/shard_map/scatter-add | solution.py:78
  175.6 1.9 reshape.291
  177.5 2.8 fusion.109
  180.3 1.9 collective-permute-start.2
  182.2 7.4 %collective-permute-start.3 = (f32[1,3,256,256]{3,2,1,0:T(8,128)}, f32[1,3,256,256]{3,2,1,0:T(8,128)}, u32[]{:S(2)}, u32[]{:S(2)}) collective-permute-start(f32[1,3,256,256]{3,2,1,0:T(8,128)} %get-tuple-element.55), channel_id=1, source_target_pairs={{1,0},{2,1},{3,2},{4,3},{5,4},{6,5},{7,6},{8,7},{9,8},{10,9},{11,1... | collective-permute-start | bytes 2359304 | tf_op jit(solution)/shard_map/ppermute | solution.py:32
  189.7 2.1 convolution_bitcast_fusion.5
  191.8 1.3 copy.38
  193.1 4.4 collective-permute-done.2
  197.6 1.5 fusion.26
  199.3 1.3 fusion.25
  200.6 1.4 copy.48
  202.0 1.3 all_to_all.54
  203.4 5.2 %broadcast_multiply_fusion.1 = (f32[1,4,256,256]{3,2,1,0:T(8,128)S(1)}, f32[1,4,256,256]{3,2,1,0:T(8,128)}) fusion(f32[1,4,256,256]{3,2,1,0:T(8,128)S(1)} %copy-done.2, f32[1,4,256,256]{3,2,1,0:T(8,128)S(1)} %fusion.25, f32[4,256,256]{2,1,0:T(8,128)} %param.15, f32[1,4,256,256]{3,2,1,0:T(8,128)} %all_to_all.54, f32[1,4,256,256]{3,2,1,0:T(8,128)} %bitcast.165), kind=kOutput, calls=%fused_computation.50 | convolution fusion | flops 808910848 | bytes 7340032 | tf_op jit(solution)/shard_map/ozyx,yw->ozwx/dot_general | solution.py:92
  209.2 63.0 %all_to_all.67 = f32[1,4,256,256]{3,1,0,2:T(4,128)S(1)} all-to-all(f32[1,4,256,256]{3,1,0,2:T(4,128)S(1)} %copy.25), channel_id=1, replica_groups=mesh['orb'=8,'grid'=64] {'grid'}, dimensions={2} | all-to-all | bytes 2097152 | tf_op jit(solution)/shard_map/all_to_all | solution.py:94
  272.8 2.1 convolution_bitcast_fusion
  274.9 1.7 copy.27
  276.6 9.6 %all-to-all-start.3 = ((f32[1,256,4,256]{3,2,0,1:T(4,128)}), f32[1,256,4,256]{3,2,0,1:T(4,128)}, u32[]{:S(2)}, u32[]{:S(2)}) async-start(f32[1,256,4,256]{3,2,0,1:T(4,128)} %copy.27), calls=%async_computation.3 | async-start | bytes 2097152 | tf_op jit(solution)/shard_map/all_to_all | solution.py:63
  286.4 2.1 collective-permute-start.4
  288.4 7.3 %collective-permute-start.5 = (f32[1,3,256,256]{3,2,1,0:T(8,128)S(1)}, f32[1,3,256,256]{3,2,1,0:T(8,128)S(1)}, u32[]{:S(2)}, u32[]{:S(2)}) collective-permute-start(f32[1,3,256,256]{3,2,1,0:T(8,128)S(1)} %get-tuple-element.58), channel_id=1, source_target_pairs={{1,0},{2,1},{3,2},{4,3},{5,4},{6,5},{7,6},{8,7},{9,8},{10,9},{11,1... | collective-permute-start | bytes 2359304 | tf_op jit(solution)/shard_map/ppermute | solution.py:22
  295.8 47.1 %collective-permute-done.4 = f32[1,3,256,256]{3,2,1,0:T(8,128)S(1)} collective-permute-done((f32[1,3,256,256]{3,2,1,0:T(8,128)S(1)}, f32[1,3,256,256]{3,2,1,0:T(8,128)S(1)}, u32[]{:S(2)}, u32[]{:S(2)}) %collective-permute-start.4) | collective-permute-done | bytes 786464 | tf_op jit(solution)/shard_map/ppermute | solution.py:20
  343.1 1.3 copy.41
  344.5 11.8 %gather_fusion.1 = f32[2048]{0:T(1024)S(1)} fusion(f32[655360]{0:T(1024)S(1)} %bitcast.160, s32[2048]{0:T(1024)S(1)} %broadcast_clamp_fusion), kind=kCustom, calls=%fused_computation.1 | custom fusion | bytes 24576 | tf_op jit(solution)/shard_map/gather | solution.py:73
  356.8 12.9 %scatter_custom_fusion.1 = f32[655360]{0:T(1024)} fusion(s32[2048]{0:T(1024)S(1)} %bitcast.174, f32[2048]{0:T(1024)S(1)} %bitcast.181, f32[]{:T(128)} %constant.158.clone.1), kind=kCustom, calls=%fused_computation.12 | custom fusion | flops 2048 | bytes 2621444 | tf_op jit(solution)/shard_map/scatter-add | solution.py:78
  369.7 2.7 reshape.296
  372.7 2.1 collective-permute-start.6
  374.7 7.3 %collective-permute-start.7 = (f32[1,3,256,256]{3,2,1,0:T(8,128)S(1)}, f32[1,3,256,256]{3,2,1,0:T(8,128)S(1)}, u32[]{:S(2)}, u32[]{:S(2)}) collective-permute-start(f32[1,3,256,256]{3,2,1,0:T(8,128)S(1)} %get-tuple-element.53), channel_id=1, source_target_pairs={{1,0},{2,1},{3,2},{4,3},{5,4},{6,5},{7,6},{8,7},{9,8},{10,9},{11,1... | collective-permute-start | bytes 2359304 | tf_op jit(solution)/shard_map/ppermute | solution.py:32
  383.3 3.1 convolution_bitcast_fusion.1
  386.4 1.1 slice.193
  387.4 2.3 collective-permute-done.6
  389.7 1.0 fusion.24
  390.7 0.7 collective-permute-done.7
  391.5 2.2 fusion.23
  393.7 2.5 copy.46
  396.2 2.6 all_to_all.61
  398.8 6.6 %fusion.21 = f32[4,256,256]{2,1,0:T(8,128)} fusion(f32[1,4,256,256]{3,2,1,0:T(8,128)S(1)} %copy-done.3, f32[1,4,256,256]{3,2,1,0:T(8,128)} %fusion.23, f32[4,256,256]{2,1,0:T(8,128)S(1)} %copy-done.4, f32[1,4,256,256]{3,2,1,0:T(8,128)S(1)} %copy-done.6, f32[]{:T(128)} %bitcast.28, f32[]{:T(128)} %bitcast.27, f32[]{:T(128)} %bitcast, ...), kind=kOutput, calls=%fused_computation.35 | convolution fusion | flops 811270144 | bytes 7340044 | tf_op jit(solution)/shard_map/dot_general | solution.py:89
  405.3 92.9 %all-reduce.2.cloned.1.call-done = f32[4,256,256]{2,1,0:T(8,128)} async-done(((f32[4,256,256]{2,1,0:T(8,128)}), f32[4,256,256]{2,1,0:T(8,128)}) %all-reduce.2.cloned.1.call-update) | async-done | bytes 1048592 | tf_op jit(solution)/shard_map/psum | solution.py:105
  498.2 2.3 broadcast_multiply_fusion
  (47 shorter events, 4.6 us)
Async XLA Ops:
  6.5 156.6 %copy-start = (f32[16,4,128]{2,1,0:T(4,128)S(1)}, f32[16,4,128]{2,1,0:T(4,128)}, u32[]{:S(2)}) copy-start(f32[16,4,128]{2,1,0:T(4,128)} %param.17) | copy-start | bytes 98308
  81.6 11.4 %copy-start.1 = (f32[1,4,256,256]{3,2,1,0:T(8,128)S(1)}, f32[1,4,256,256]{3,2,1,0:T(8,128)}, u32[]{:S(2)}) copy-start(f32[1,4,256,256]{3,2,1,0:T(8,128)} %param.14) | copy-start | bytes 3145732
  83.3 20.0 %copy-start.7 = (s32[16,2,128]{2,1,0:T(2,128)S(1)}, s32[16,2,128]{2,1,0:T(2,128)}, u32[]{:S(2)}) copy-start(s32[16,2,128]{2,1,0:T(2,128)} %param.16) | copy-start | bytes 49156
  83.3 117.3 %all-to-all-start.1 = ((f32[1,256,4,256]{3,2,0,1:T(4,128)}), f32[1,256,4,256]{3,2,0,1:T(4,128)}, u32[]{:S(2)}, u32[]{:S(2)}) async-start(f32[1,256,4,256]{3,2,0,1:T(4,128)} %copy.22), calls=%async_computation.1 | async-start | bytes 2097152 | tf_op jit(solution)/shard_map/all_to_all | solution.py:63
  94.1 55.6 %collective-permute-start = (f32[1,3,256,256]{3,2,1,0:T(8,128)}, f32[1,3,256,256]{3,2,1,0:T(8,128)S(1)}, u32[]{:S(2)}, u32[]{:S(2)}) collective-permute-start(f32[1,3,256,256]{3,2,1,0:T(8,128)} %get-tuple-element.59), channel_id=1, source_target_pairs={{0,1},{1,2},{2,3},{3,4},{4,5},{5,6},{6,7},{7,8},{8,9},{9,10},{10,1... | collective-permute-start | bytes 2359304 | tf_op jit(solution)/shard_map/ppermute | solution.py:20
  96.2 53.6 %collective-permute-start.1 = (f32[1,3,256,256]{3,2,1,0:T(8,128)S(1)}, f32[1,3,256,256]{3,2,1,0:T(8,128)S(1)}, u32[]{:S(2)}, u32[]{:S(2)}) collective-permute-start(f32[1,3,256,256]{3,2,1,0:T(8,128)S(1)} %get-tuple-element.60), channel_id=1, source_target_pairs={{1,0},{2,1},{3,2},{4,3},{5,4},{6,5},{7,6},{8,7},{9,8},{10,9},{11,1... | collective-permute-start | bytes 2359304 | tf_op jit(solution)/shard_map/ppermute | solution.py:22
  151.3 12.1 %copy-start.9 = (f32[4]{0:T(128)S(1)}, f32[4]{0:T(128)}, u32[]{:S(2)}) copy-start(f32[4]{0:T(128)} %param.18) | copy-start | bytes 52
  177.5 12.2 %copy-start.2 = (f32[1,4,256,256]{3,2,1,0:T(8,128)S(1)}, f32[1,4,256,256]{3,2,1,0:T(8,128)}, u32[]{:S(2)}) copy-start(f32[1,4,256,256]{3,2,1,0:T(8,128)} %param.14) | copy-start | bytes 3145732
  180.3 17.2 %collective-permute-start.2 = (f32[1,3,256,256]{3,2,1,0:T(8,128)}, f32[1,3,256,256]{3,2,1,0:T(8,128)}, u32[]{:S(2)}, u32[]{:S(2)}) collective-permute-start(f32[1,3,256,256]{3,2,1,0:T(8,128)} %get-tuple-element.56), channel_id=1, source_target_pairs={{63,0},{0,1},{1,2},{2,3},{3,4},{4,5},{5,6},{6,7},{7,8},{8,9},{9,10... | collective-permute-start | bytes 2359304 | tf_op jit(solution)/shard_map/ppermute | solution.py:32
  182.2 17.1 %collective-permute-start.3 = (f32[1,3,256,256]{3,2,1,0:T(8,128)}, f32[1,3,256,256]{3,2,1,0:T(8,128)}, u32[]{:S(2)}, u32[]{:S(2)}) collective-permute-start(f32[1,3,256,256]{3,2,1,0:T(8,128)} %get-tuple-element.55), channel_id=1, source_target_pairs={{1,0},{2,1},{3,2},{4,3},{5,4},{6,5},{7,6},{8,7},{9,8},{10,9},{11,1... | collective-permute-start | bytes 2359304 | tf_op jit(solution)/shard_map/ppermute | solution.py:32
  191.8 5.8 %slice-start = ((f32[1,10,256,256]{3,2,1,0:T(8,128)}), f32[1,4,256,256]{3,2,1,0:T(8,128)S(1)}, s32[]{:S(2)}) async-start(f32[1,10,256,256]{3,2,1,0:T(8,128)} %reshape.291), calls=%async_computation.5 | async-start | bytes 2097152 | tf_op jit(solution)/shard_map/slice | solution.py:83
  276.6 117.1 %all-to-all-start.3 = ((f32[1,256,4,256]{3,2,0,1:T(4,128)}), f32[1,256,4,256]{3,2,0,1:T(4,128)}, u32[]{:S(2)}, u32[]{:S(2)}) async-start(f32[1,256,4,256]{3,2,0,1:T(4,128)} %copy.27), calls=%async_computation.3 | async-start | bytes 2097152 | tf_op jit(solution)/shard_map/all_to_all | solution.py:63
  286.2 212.0 %all-reduce.2.cloned.1.call-start = ((), (), s32[]{:S(2)}) async-start(), calls=%async_computation.4 | async-start | bytes 2097152 | tf_op jit(solution)/shard_map/psum | solution.py:105
  286.4 56.5 %collective-permute-start.4 = (f32[1,3,256,256]{3,2,1,0:T(8,128)S(1)}, f32[1,3,256,256]{3,2,1,0:T(8,128)S(1)}, u32[]{:S(2)}, u32[]{:S(2)}) collective-permute-start(f32[1,3,256,256]{3,2,1,0:T(8,128)S(1)} %get-tuple-element.57), channel_id=1, source_target_pairs={{0,1},{1,2},{2,3},{3,4},{4,5},{5,6},{6,7},{7,8},{8,9},{9,10},{10,1... | collective-permute-start | bytes 2359304 | tf_op jit(solution)/shard_map/ppermute | solution.py:20
  288.4 54.4 %collective-permute-start.5 = (f32[1,3,256,256]{3,2,1,0:T(8,128)S(1)}, f32[1,3,256,256]{3,2,1,0:T(8,128)S(1)}, u32[]{:S(2)}, u32[]{:S(2)}) collective-permute-start(f32[1,3,256,256]{3,2,1,0:T(8,128)S(1)} %get-tuple-element.58), channel_id=1, source_target_pairs={{1,0},{2,1},{3,2},{4,3},{5,4},{6,5},{7,6},{8,7},{9,8},{10,9},{11,1... | collective-permute-start | bytes 2359304 | tf_op jit(solution)/shard_map/ppermute | solution.py:22
  372.5 9.5 %copy-start.8 = (f32[3]{0:T(128)S(1)}, f32[3]{0:T(128)}, u32[]{:S(2)}) copy-start(f32[3]{0:T(128)} %param.19) | copy-start | bytes 40
  372.5 10.8 %copy-start.5 = (f32[1,4,256,256]{3,2,1,0:T(8,128)S(1)}, f32[1,4,256,256]{3,2,1,0:T(8,128)}, u32[]{:S(2)}) copy-start(f32[1,4,256,256]{3,2,1,0:T(8,128)} %get-tuple-element.65) | copy-start | bytes 3145732
  372.7 17.1 %collective-permute-start.6 = (f32[1,3,256,256]{3,2,1,0:T(8,128)S(1)}, f32[1,3,256,256]{3,2,1,0:T(8,128)S(1)}, u32[]{:S(2)}, u32[]{:S(2)}) collective-permute-start(f32[1,3,256,256]{3,2,1,0:T(8,128)S(1)} %get-tuple-element.54), channel_id=1, source_target_pairs={{63,0},{0,1},{1,2},{2,3},{3,4},{4,5},{5,6},{6,7},{7,8},{8,9},{9,10... | collective-permute-start | bytes 2359304 | tf_op jit(solution)/shard_map/ppermute | solution.py:32
  374.7 16.8 %collective-permute-start.7 = (f32[1,3,256,256]{3,2,1,0:T(8,128)S(1)}, f32[1,3,256,256]{3,2,1,0:T(8,128)S(1)}, u32[]{:S(2)}, u32[]{:S(2)}) collective-permute-start(f32[1,3,256,256]{3,2,1,0:T(8,128)S(1)} %get-tuple-element.53), channel_id=1, source_target_pairs={{1,0},{2,1},{3,2},{4,3},{5,4},{6,5},{7,6},{8,7},{9,8},{10,9},{11,1... | collective-permute-start | bytes 2359304 | tf_op jit(solution)/shard_map/ppermute | solution.py:32
  393.6 5.1 %copy-start.3 = (f32[1,4,256,256]{3,2,1,0:T(8,128)S(1)}, f32[1,4,256,256]{3,2,1,0:T(8,128)}, u32[]{:S(2)}) copy-start(f32[1,4,256,256]{3,2,1,0:T(8,128)} %param.14) | copy-start | bytes 3145732
  393.6 5.1 %copy-start.4 = (f32[4,256,256]{2,1,0:T(8,128)S(1)}, f32[4,256,256]{2,1,0:T(8,128)}, u32[]{:S(2)}) copy-start(f32[4,256,256]{2,1,0:T(8,128)} %param.15) | copy-start | bytes 3145732
  393.7 5.1 %copy-start.6 = (f32[1,4,256,256]{3,2,1,0:T(8,128)S(1)}, f32[1,4,256,256]{3,2,1,0:T(8,128)}, u32[]{:S(2)}) copy-start(f32[1,4,256,256]{3,2,1,0:T(8,128)} %get-tuple-element.65) | copy-start | bytes 3145732
Sparse Core Ops, SparseCore 0:
  405.5 92.7 all-reduce.1
where the time goes:
time: 508 us; the launch traced here: 507 us
  waiting for transfers between devices  194 us (38%)
  blocking collectives  134 us (26%)
  starting transfers between devices  56.7 us (11%)
  local copies, waits for them, and re-layouts  52.9 us (10%)
  other arithmetic  33.6 us (7%)
  matrix products  22.1 us (4%)
  between operations  14.4 us (3%)
    all_to_all x2, blocking collectives, apply_hamiltonian(): lax.all_to_all(vector, 'grid', split_axis=2, concat_axis=1, tiled=True)  134 us
    ppermute x2, waiting for transfers between devices, with_halo(): lax.ppermute(tail, axis, [(i, (i + 1) % count) for i in range(count)])  93.5 us
    psum x1, waiting for transfers between devices, local(): density = lax.psum(group_density, 'orb')  92.9 us
    scatter-add x2, other arithmetic, nonlocal_term(): jnp.zeros_like(flattened).at[:, ghost_index].add(spread)  24.9 us
    gather x2, local copies, waits for them, and re-layouts, nonlocal_term(): values = flattened[:, ghost_index].reshape(orb_count, per_dev, -1)  23.6 us
    all_to_all x2, starting transfers between devices, along_z(): lax.all_to_all(turned, 'grid', split_axis=1, concat_axis=2, tiled=True)  19.4 us
    ppermute x4, starting transfers between devices, from_behind(): return lax.ppermute(block, axis, route)  18.7 us
    ppermute x2, starting transfers between devices, with_halo(): lax.ppermute(head, axis, [((i + 1) % count, i) for i in range(count)])  14.5 us
  transfers between devices with their start and end apart: 11, of which 7 were waited for; matrix products, arithmetic and copies ran while one was open for 15% of the time, Pallas kernels for 0%

commit v1 on v0

--- a/solution.py
+++ b/solution.py
@@ -3,11 +3,18 @@
 import jax.numpy as jnp
 from jax import lax
 from jax.sharding import PartitionSpec as P
+from jax.lax import all_to_all, psum
 
 REACH = 3
 PRECISE = lax.Precision.HIGHEST
 CENTRE = 2.0
 HALF_RANGE = 4.0
+sizes_feed = lambda content, named_axis: jnp.concatenate(
+    all_to_all(
+        jnp.stack(jnp.split(content, psum(1, axis_name=named_axis), 1), 0), named_axis, 0, 0
+    ),
+    2,
+)
 
 
 def with_halo(cells, sides, width):
@@ -60,7 +67,7 @@
 
     def along_z(columns):
         turned = jnp.einsum("ozyx,zw->owyx", columns, kinetic_z, precision=PRECISE)
-        return lax.all_to_all(turned, "grid", split_axis=1, concat_axis=2, tiled=True)
+        return sizes_feed(turned, "grid")
 
     z_glob = sphere_cells[:, 0, :]
     in_plane = sphere_cells[:, 1, :]

time: 508 us -> 575 us (1.13)
  local copies, waits for them, and re-layouts: 52.9 us -> 119 us
    unnamed x23 -> x151, local copies, waits for them, and re-layouts: 4.65 us -> 80.9 us
    all_to_all x4 -> x0, local copies, waits for them, and re-layouts: 7.83 us -> none  [along_z(): lax.all_to_all(turned, 'grid', split_axis=1, concat_axis=2, tiled=True)]
  transfers between devices with their start and end apart: 11 -> 11, of which waited for: 7 -> 6; matrix products, arithmetic and copies ran while one was open for 15% -> 13% of each run, Pallas kernels for 0% -> 0%
where the time goes in v1:
time: 575 us; the launch traced here: 574 us
  waiting for transfers between devices  193 us (34%)
  blocking collectives  134 us (23%)
  local copies, waits for them, and re-layouts  119 us (21%)
  starting transfers between devices  56.8 us (10%)
  other arithmetic  34.7 us (6%)
  matrix products  22.1 us (4%)
  between operations  14.4 us (3%)
    all_to_all x2, blocking collectives, apply_hamiltonian(): lax.all_to_all(vector, 'grid', split_axis=2, concat_axis=1, tiled=True)  134 us
    ppermute x2, waiting for transfers between devices, with_halo(): lax.ppermute(tail, axis, [(i, (i + 1) % count) for i in range(count)])  93.5 us
    psum x1, waiting for transfers between devices, local(): density = lax.psum(group_density, 'orb')  92.4 us
    unnamed x151, local copies, waits for them, and re-layouts  80.9 us
    scatter-add x2, other arithmetic, nonlocal_term(): jnp.zeros_like(flattened).at[:, ghost_index].add(spread)  24.9 us
    gather x2, local copies, waits for them, and re-layouts, nonlocal_term(): values = flattened[:, ghost_index].reshape(orb_count, per_dev, -1)  23.6 us
    all_to_all x2, starting transfers between devices, all_to_all(jnp.stack(jnp.split(content, psum(1, axis_name=named_axis), 1)...  19.4 us
    ppermute x4, starting transfers between devices, from_behind(): return lax.ppermute(block, axis, route)  18.8 us
  transfers between devices with their start and end apart: 11, of which 6 were waited for; matrix products, arithmetic and copies ran while one was open for 13% of the time, Pallas kernels for 0%

profile of v1, /device:TPU:4, one launch (start us, length us, event | category | flops | bytes accessed | tf_op | source)
XLA Modules:
  0.0 573.9 jit_solution(2281132660657755700)
XLA Ops:
  6.5 1.9 copy.20
  8.4 70.6 %all_to_all.40 = f32[1,4,256,256]{3,1,0,2:T(4,128)S(1)} all-to-all(f32[1,4,256,256]{3,1,0,2:T(4,128)S(1)} %copy.20), channel_id=1, replica_groups=mesh['orb'=8,'grid'=64] {'grid'}, dimensions={2} | all-to-all | bytes 2097152 | tf_op jit(solution)/shard_map/all_to_all | solution.py:101
  79.6 2.1 convolution_bitcast_fusion.3
  82.3 0.6 constant_dynamic-update-slice_fusion.62
  83.5 0.6 constant_dynamic-update-slice_fusion.60
  120.6 9.8 %all-to-all-start.1 = ((f32[64,1,4,4,256]{4,2,3,1,0:T(4,128)}), f32[64,1,4,4,256]{4,2,3,1,0:T(4,128)}, u32[]{:S(2)}, u32[]{:S(2)}) async-start(f32[64,1,4,4,256]{4,2,3,1,0:T(4,128)} %constant_dynamic-update-slice_fusion), calls=%async_computation.1 | async-start | bytes 2097152 | tf_op jit(solution)/shard_map/all_to_all | solution.py:13
  130.4 1.0 fusion.111
  131.4 2.0 collective-permute-start
  133.5 7.1 %collective-permute-start.1 = (f32[1,3,256,256]{3,2,1,0:T(8,128)S(1)}, f32[1,3,256,256]{3,2,1,0:T(8,128)S(1)}, u32[]{:S(2)}, u32[]{:S(2)}) collective-permute-start(f32[1,3,256,256]{3,2,1,0:T(8,128)S(1)} %get-tuple-element.60), channel_id=1, source_target_pairs={{1,0},{2,1},{3,2},{4,3},{5,4},{6,5},{7,6},{8,7},{9,8},{10,9},{11,1... | collective-permute-start | bytes 2359304 | tf_op jit(solution)/shard_map/ppermute | solution.py:29
  140.7 46.4 %collective-permute-done = f32[1,3,256,256]{3,2,1,0:T(8,128)S(1)} collective-permute-done((f32[1,3,256,256]{3,2,1,0:T(8,128)}, f32[1,3,256,256]{3,2,1,0:T(8,128)S(1)}, u32[]{:S(2)}, u32[]{:S(2)}) %collective-permute-start) | collective-permute-done | bytes 786464 | tf_op jit(solution)/shard_map/ppermute | solution.py:27
  187.3 1.3 copy.40
  188.6 11.8 %gather_fusion = f32[2048]{0:T(1024)S(1)} fusion(f32[655360]{0:T(1024)S(1)} %bitcast.671, s32[2048]{0:T(1024)S(1)} %broadcast_clamp_fusion), kind=kCustom, calls=%fused_computation | custom fusion | bytes 24576 | tf_op jit(solution)/shard_map/gather | solution.py:80
  201.0 11.9 %scatter_custom_fusion = f32[655360]{0:T(1024)S(1)} fusion(s32[2048]{0:T(1024)S(1)} %bitcast.681, f32[2048]{0:T(1024)S(1)} %bitcast.690, f32[]{:T(128)} %constant.158.clone.1), kind=kCustom, calls=%fused_computation.14 | custom fusion | flops 2048 | bytes 2621444 | tf_op jit(solution)/shard_map/scatter-add | solution.py:85
  212.9 1.9 reshape.305
  214.8 2.8 fusion.109
  217.6 1.9 collective-permute-start.2
  219.5 7.4 %collective-permute-start.3 = (f32[1,3,256,256]{3,2,1,0:T(8,128)}, f32[1,3,256,256]{3,2,1,0:T(8,128)}, u32[]{:S(2)}, u32[]{:S(2)}) collective-permute-start(f32[1,3,256,256]{3,2,1,0:T(8,128)} %get-tuple-element.55), channel_id=1, source_target_pairs={{1,0},{2,1},{3,2},{4,3},{5,4},{6,5},{7,6},{8,7},{9,8},{10,9},{11,1... | collective-permute-start | bytes 2359304 | tf_op jit(solution)/shard_map/ppermute | solution.py:39
  227.0 2.1 convolution_bitcast_fusion.5
  229.1 1.3 copy.36
  230.4 4.4 collective-permute-done.2
  234.9 1.5 fusion.26
  236.6 1.3 fusion.25
  237.9 5.3 broadcast_multiply_fusion.1
  243.2 0.7 copy.24
  243.9 63.0 %all_to_all.41 = f32[1,4,256,256]{3,1,0,2:T(4,128)S(1)} all-to-all(f32[1,4,256,256]{3,1,0,2:T(4,128)S(1)} %copy.24), channel_id=1, replica_groups=mesh['orb'=8,'grid'=64] {'grid'}, dimensions={2} | all-to-all | bytes 2097152 | tf_op jit(solution)/shard_map/all_to_all | solution.py:101
  307.5 2.1 convolution_bitcast_fusion
  317.4 0.6 constant_dynamic-update-slice_fusion.114
  334.3 0.6 constant_dynamic-update-slice_fusion.86
  336.1 0.6 constant_dynamic-update-slice_fusion.83
  339.1 0.6 constant_dynamic-update-slice_fusion.78
  348.2 9.6 %all-to-all-start.3 = ((f32[64,1,4,4,256]{4,2,3,1,0:T(4,128)}), f32[64,1,4,4,256]{4,2,3,1,0:T(4,128)}, u32[]{:S(2)}, u32[]{:S(2)}) async-start(f32[64,1,4,4,256]{4,2,3,1,0:T(4,128)} %constant_dynamic-update-slice_fusion.64), calls=%async_computation.3 | async-start | bytes 2097152 | tf_op jit(solution)/shard_map/all_to_all | solution.py:13
  358.0 2.1 collective-permute-start.4
  360.1 7.3 %collective-permute-start.5 = (f32[1,3,256,256]{3,2,1,0:T(8,128)S(1)}, f32[1,3,256,256]{3,2,1,0:T(8,128)S(1)}, u32[]{:S(2)}, u32[]{:S(2)}) collective-permute-start(f32[1,3,256,256]{3,2,1,0:T(8,128)S(1)} %get-tuple-element.58), channel_id=1, source_target_pairs={{1,0},{2,1},{3,2},{4,3},{5,4},{6,5},{7,6},{8,7},{9,8},{10,9},{11,1... | collective-permute-start | bytes 2359304 | tf_op jit(solution)/shard_map/ppermute | solution.py:29
  367.4 47.1 %collective-permute-done.4 = f32[1,3,256,256]{3,2,1,0:T(8,128)S(1)} collective-permute-done((f32[1,3,256,256]{3,2,1,0:T(8,128)S(1)}, f32[1,3,256,256]{3,2,1,0:T(8,128)S(1)}, u32[]{:S(2)}, u32[]{:S(2)}) %collective-permute-start.4) | collective-permute-done | bytes 786464 | tf_op jit(solution)/shard_map/ppermute | solution.py:27
  414.7 1.3 copy.41
  416.1 11.8 %gather_fusion.1 = f32[2048]{0:T(1024)S(1)} fusion(f32[655360]{0:T(1024)S(1)} %bitcast.670, s32[2048]{0:T(1024)S(1)} %broadcast_clamp_fusion), kind=kCustom, calls=%fused_computation.1 | custom fusion | bytes 24576 | tf_op jit(solution)/shard_map/gather | solution.py:80
  428.4 12.9 %scatter_custom_fusion.1 = f32[655360]{0:T(1024)} fusion(s32[2048]{0:T(1024)S(1)} %bitcast.682, f32[2048]{0:T(1024)S(1)} %bitcast.689, f32[]{:T(128)} %constant.158.clone.1), kind=kCustom, calls=%fused_computation.12 | custom fusion | flops 2048 | bytes 2621444 | tf_op jit(solution)/shard_map/scatter-add | solution.py:85
  441.3 2.7 reshape.312
  444.3 2.2 collective-permute-start.6
  446.5 7.3 %collective-permute-start.7 = (f32[1,3,256,256]{3,2,1,0:T(8,128)S(1)}, f32[1,3,256,256]{3,2,1,0:T(8,128)S(1)}, u32[]{:S(2)}, u32[]{:S(2)}) collective-permute-start(f32[1,3,256,256]{3,2,1,0:T(8,128)S(1)} %get-tuple-element.53), channel_id=1, source_target_pairs={{1,0},{2,1},{3,2},{4,3},{5,4},{6,5},{7,6},{8,7},{9,8},{10,9},{11,1... | collective-permute-start | bytes 2359304 | tf_op jit(solution)/shard_map/ppermute | solution.py:39
  454.9 3.1 convolution_bitcast_fusion.1
  458.0 1.1 slice.193
  459.1 2.4 collective-permute-done.6
  461.5 2.1 fusion.24
  463.6 2.1 fusion.23
  465.8 6.5 %fusion.21 = f32[4,256,256]{2,1,0:T(8,128)} fusion(f32[1,4,256,256]{3,2,1,0:T(8,128)S(1)} %copy-done.3, f32[1,4,256,256]{3,2,1,0:T(8,128)} %fusion.23, f32[4,256,256]{2,1,0:T(8,128)S(1)} %copy-done.5, f32[1,4,256,256]{3,2,1,0:T(8,128)S(1)} %copy-done.7, f32[]{:T(128)} %bitcast.92, f32[]{:T(128)} %bitcast.91, f32[]{:T(128)} %bitcast, ...), kind=kOutput, calls=%fused_computation.35 | convolution fusion | flops 811270144 | bytes 7340044 | tf_op jit(solution)/shard_map/dot_general | solution.py:96
  472.3 92.4 %all-reduce.2.cloned.1.call-done = f32[4,256,256]{2,1,0:T(8,128)} async-done(((f32[4,256,256]{2,1,0:T(8,128)}), f32[4,256,256]{2,1,0:T(8,128)}) %all-reduce.2.cloned.1.call-update) | async-done | bytes 1048592 | tf_op jit(solution)/shard_map/psum | solution.py:112
  564.8 2.3 broadcast_multiply_fusion
  (171 shorter events, 77.7 us)
Async XLA Ops:
  6.5 193.9 %copy-start = (f32[16,4,128]{2,1,0:T(4,128)S(1)}, f32[16,4,128]{2,1,0:T(4,128)}, u32[]{:S(2)}) copy-start(f32[16,4,128]{2,1,0:T(4,128)} %param.17) | copy-start | bytes 98308
  81.6 48.8 %copy-start.1 = (f32[1,4,256,256]{3,2,1,0:T(8,128)S(1)}, f32[1,4,256,256]{3,2,1,0:T(8,128)}, u32[]{:S(2)}) copy-start(f32[1,4,256,256]{3,2,1,0:T(8,128)} %param.14) | copy-start | bytes 3145732
  120.6 20.0 %copy-start.8 = (s32[16,2,128]{2,1,0:T(2,128)S(1)}, s32[16,2,128]{2,1,0:T(2,128)}, u32[]{:S(2)}) copy-start(s32[16,2,128]{2,1,0:T(2,128)} %param.16) | copy-start | bytes 49156
  120.6 117.3 %all-to-all-start.1 = ((f32[64,1,4,4,256]{4,2,3,1,0:T(4,128)}), f32[64,1,4,4,256]{4,2,3,1,0:T(4,128)}, u32[]{:S(2)}, u32[]{:S(2)}) async-start(f32[64,1,4,4,256]{4,2,3,1,0:T(4,128)} %constant_dynamic-update-slice_fusion), calls=%async_computation.1 | async-start | bytes 2097152 | tf_op jit(solution)/shard_map/all_to_all | solution.py:13
  131.4 55.6 %collective-permute-start = (f32[1,3,256,256]{3,2,1,0:T(8,128)}, f32[1,3,256,256]{3,2,1,0:T(8,128)S(1)}, u32[]{:S(2)}, u32[]{:S(2)}) collective-permute-start(f32[1,3,256,256]{3,2,1,0:T(8,128)} %get-tuple-element.59), channel_id=1, source_target_pairs={{0,1},{1,2},{2,3},{3,4},{4,5},{5,6},{6,7},{7,8},{8,9},{9,10},{10,1... | collective-permute-start | bytes 2359304 | tf_op jit(solution)/shard_map/ppermute | solution.py:27
  133.5 53.6 %collective-permute-start.1 = (f32[1,3,256,256]{3,2,1,0:T(8,128)S(1)}, f32[1,3,256,256]{3,2,1,0:T(8,128)S(1)}, u32[]{:S(2)}, u32[]{:S(2)}) collective-permute-start(f32[1,3,256,256]{3,2,1,0:T(8,128)S(1)} %get-tuple-element.60), channel_id=1, source_target_pairs={{1,0},{2,1},{3,2},{4,3},{5,4},{6,5},{7,6},{8,7},{9,8},{10,9},{11,1... | collective-permute-start | bytes 2359304 | tf_op jit(solution)/shard_map/ppermute | solution.py:29
  188.6 12.1 %copy-start.10 = (f32[4]{0:T(128)S(1)}, f32[4]{0:T(128)}, u32[]{:S(2)}) copy-start(f32[4]{0:T(128)} %param.18) | copy-start | bytes 52
  214.8 12.2 %copy-start.2 = (f32[1,4,256,256]{3,2,1,0:T(8,128)S(1)}, f32[1,4,256,256]{3,2,1,0:T(8,128)}, u32[]{:S(2)}) copy-start(f32[1,4,256,256]{3,2,1,0:T(8,128)} %param.14) | copy-start | bytes 3145732
  217.6 17.2 %collective-permute-start.2 = (f32[1,3,256,256]{3,2,1,0:T(8,128)}, f32[1,3,256,256]{3,2,1,0:T(8,128)}, u32[]{:S(2)}, u32[]{:S(2)}) collective-permute-start(f32[1,3,256,256]{3,2,1,0:T(8,128)} %get-tuple-element.56), channel_id=1, source_target_pairs={{63,0},{0,1},{1,2},{2,3},{3,4},{4,5},{5,6},{6,7},{7,8},{8,9},{9,10... | collective-permute-start | bytes 2359304 | tf_op jit(solution)/shard_map/ppermute | solution.py:39
  219.5 17.1 %collective-permute-start.3 = (f32[1,3,256,256]{3,2,1,0:T(8,128)}, f32[1,3,256,256]{3,2,1,0:T(8,128)}, u32[]{:S(2)}, u32[]{:S(2)}) collective-permute-start(f32[1,3,256,256]{3,2,1,0:T(8,128)} %get-tuple-element.55), channel_id=1, source_target_pairs={{1,0},{2,1},{3,2},{4,3},{5,4},{6,5},{7,6},{8,7},{9,8},{10,9},{11,1... | collective-permute-start | bytes 2359304 | tf_op jit(solution)/shard_map/ppermute | solution.py:39
  229.1 5.8 %slice-start = ((f32[1,10,256,256]{3,2,1,0:T(8,128)}), f32[1,4,256,256]{3,2,1,0:T(8,128)S(1)}, s32[]{:S(2)}) async-start(f32[1,10,256,256]{3,2,1,0:T(8,128)} %reshape.305), calls=%async_computation.5 | async-start | bytes 2097152 | tf_op jit(solution)/shard_map/slice | solution.py:90
  348.2 117.6 %all-to-all-start.3 = ((f32[64,1,4,4,256]{4,2,3,1,0:T(4,128)}), f32[64,1,4,4,256]{4,2,3,1,0:T(4,128)}, u32[]{:S(2)}, u32[]{:S(2)}) async-start(f32[64,1,4,4,256]{4,2,3,1,0:T(4,128)} %constant_dynamic-update-slice_fusion.64), calls=%async_computation.3 | async-start | bytes 2097152 | tf_op jit(solution)/shard_map/all_to_all | solution.py:13
  357.8 207.0 %all-reduce.2.cloned.1.call-start = ((), (), s32[]{:S(2)}) async-start(), calls=%async_computation.4 | async-start | bytes 2097152 | tf_op jit(solution)/shard_map/psum | solution.py:112
  358.0 56.5 %collective-permute-start.4 = (f32[1,3,256,256]{3,2,1,0:T(8,128)S(1)}, f32[1,3,256,256]{3,2,1,0:T(8,128)S(1)}, u32[]{:S(2)}, u32[]{:S(2)}) collective-permute-start(f32[1,3,256,256]{3,2,1,0:T(8,128)S(1)} %get-tuple-element.57), channel_id=1, source_target_pairs={{0,1},{1,2},{2,3},{3,4},{4,5},{5,6},{6,7},{7,8},{8,9},{9,10},{10,1... | collective-permute-start | bytes 2359304 | tf_op jit(solution)/shard_map/ppermute | solution.py:27
  360.1 54.4 %collective-permute-start.5 = (f32[1,3,256,256]{3,2,1,0:T(8,128)S(1)}, f32[1,3,256,256]{3,2,1,0:T(8,128)S(1)}, u32[]{:S(2)}, u32[]{:S(2)}) collective-permute-start(f32[1,3,256,256]{3,2,1,0:T(8,128)S(1)} %get-tuple-element.58), channel_id=1, source_target_pairs={{1,0},{2,1},{3,2},{4,3},{5,4},{6,5},{7,6},{8,7},{9,8},{10,9},{11,1... | collective-permute-start | bytes 2359304 | tf_op jit(solution)/shard_map/ppermute | solution.py:29
  444.1 13.9 %copy-start.4 = (f32[1,10,256,256]{3,2,1,0:T(8,128)}, f32[1,10,256,256]{3,2,1,0:T(8,128)S(1)}, u32[]{:S(2)}) copy-start(f32[1,10,256,256]{3,2,1,0:T(8,128)S(1)} %reshape.312) | copy-start | bytes 7864324
  444.1 9.7 %copy-start.9 = (f32[3]{0:T(128)S(1)}, f32[3]{0:T(128)}, u32[]{:S(2)}) copy-start(f32[3]{0:T(128)} %param.19) | copy-start | bytes 40
  444.1 10.8 %copy-start.6 = (f32[1,4,256,256]{3,2,1,0:T(8,128)S(1)}, f32[1,4,256,256]{3,2,1,0:T(8,128)}, u32[]{:S(2)}) copy-start(f32[1,4,256,256]{3,2,1,0:T(8,128)} %get-tuple-element.65) | copy-start | bytes 3145732
  444.3 17.2 %collective-permute-start.6 = (f32[1,3,256,256]{3,2,1,0:T(8,128)S(1)}, f32[1,3,256,256]{3,2,1,0:T(8,128)S(1)}, u32[]{:S(2)}, u32[]{:S(2)}) collective-permute-start(f32[1,3,256,256]{3,2,1,0:T(8,128)S(1)} %get-tuple-element.54), channel_id=1, source_target_pairs={{63,0},{0,1},{1,2},{2,3},{3,4},{4,5},{5,6},{6,7},{7,8},{8,9},{9,10... | collective-permute-start | bytes 2359304 | tf_op jit(solution)/shard_map/ppermute | solution.py:39
  446.5 17.1 %collective-permute-start.7 = (f32[1,3,256,256]{3,2,1,0:T(8,128)S(1)}, f32[1,3,256,256]{3,2,1,0:T(8,128)S(1)}, u32[]{:S(2)}, u32[]{:S(2)}) collective-permute-start(f32[1,3,256,256]{3,2,1,0:T(8,128)S(1)} %get-tuple-element.53), channel_id=1, source_target_pairs={{1,0},{2,1},{3,2},{4,3},{5,4},{6,5},{7,6},{8,7},{9,8},{10,9},{11,1... | collective-permute-start | bytes 2359304 | tf_op jit(solution)/shard_map/ppermute | solution.py:39
  459.0 6.7 %copy-start.3 = (f32[1,4,256,256]{3,2,1,0:T(8,128)S(1)}, f32[1,4,256,256]{3,2,1,0:T(8,128)}, u32[]{:S(2)}) copy-start(f32[1,4,256,256]{3,2,1,0:T(8,128)} %param.14) | copy-start | bytes 3145732
  459.1 6.7 %copy-start.5 = (f32[4,256,256]{2,1,0:T(8,128)S(1)}, f32[4,256,256]{2,1,0:T(8,128)}, u32[]{:S(2)}) copy-start(f32[4,256,256]{2,1,0:T(8,128)} %param.15) | copy-start | bytes 3145732
  459.1 6.7 %copy-start.7 = (f32[1,4,256,256]{3,2,1,0:T(8,128)S(1)}, f32[1,4,256,256]{3,2,1,0:T(8,128)}, u32[]{:S(2)}) copy-start(f32[1,4,256,256]{3,2,1,0:T(8,128)} %get-tuple-element.65) | copy-start | bytes 3145732
Sparse Core Ops, SparseCore 0:
  472.5 92.2 all-reduce.1
